TPU v7x, 512 devices: a whole 4x8x8 slice. The times are simulated.
512 devices in a mesh: tm: 128 (over z, y, core), swath: 4 (over x).
Axes of the slice: x: 4, y: 8, z: 8, core: 2. Of those that a mesh axis runs over, the one named last changes fastest.
Arguments:
- design: bfloat16 [128, 2048, 512], P('tm', 'swath'), may hold values from -6 to 6
- process: bfloat16 [128, 512, 512], P('tm', 'swath')
- prior_prec: float32 [128, 512], P('tm', 'swath'), may hold values from 0.05 to 0.5
- routes: int32 [128, 16], P('tm', 'swath'), may hold values from -1 to 127, as said below
- counts: int32 [128, 4], P('tm', 'swath'), may hold values from 1 to 4
Outputs:
- reduced_diag: float32 [128, 512, 512], P('tm', 'swath')
- reduced_coupling: float32 [128, 512, 512], P('tm', 'swath')
Inputs may be any that keep to these rules, and one draw needn't show every extreme that they name: `routes`: each value is the holder's own time block i or i + 1, or -1 only where i + 1 would be 128; of one holder's 4 blocks, exactly 2 name i and the others i + 1 or -1.
All inputs are finite; a program needn't handle non-finite values.
Results may differ from a plain program's by a relative error of at most 0.00073.
Values may be sent and summed in bfloat16 or wider, within the bound.
No kernel may reach another device: no remote copies, remote signals or barrier semaphores. Data moves between devices by JAX's collectives and lax.ppermute only.
A program may use at most 64 MiB of HBM per device.

v0:
```python
import jax
import jax.numpy as jnp
from jax import lax
from jax.sharding import PartitionSpec as P

LEVELS = 3


def passed_along(block, axis, distance):
    devices = range(lax.axis_size(axis))
    route = [(i - distance, i) for i in devices if i - distance in devices]
    return lax.ppermute(block, axis, route)


def tri_solve(factor, right):
    return lax.linalg.triangular_solve(factor, right, left_side=True, lower=True)


def inner_rows(left_side, right_side):
    return lax.dot_general(
        left_side,
        right_side,
        (((0,), (0,)), ((), ())),
        precision=lax.Precision.HIGHEST,
        preferred_element_type=jnp.float32,
    )


def compact(scaled, wanted, slot_count):
    sort_key = jnp.where(wanted, 0, 1).astype(jnp.int32)
    picked = jnp.argsort(sort_key, stable=True)[:slot_count]
    kept = jnp.take(sort_key, picked) == 0
    return jnp.where(kept[:, None, None], scaled[picked], 0.0).astype(jnp.bfloat16)


def shards(design, process, prior_prec, routes, counts):
    row_count = process.shape[1]
    order_size = process.shape[2]
    time_count = lax.axis_size("tm")
    my_time = lax.axis_index("tm")
    swath_index = lax.axis_index("swath")
    block_count = routes.shape[1]
    slot_count = block_count // 2
    block_rows = design.shape[1] // block_count
    total_slots = 2 * slot_count * block_rows * lax.axis_size("swath")
    row_start = swath_index * row_count
    raw_rows = design[0].reshape(block_count, block_rows, order_size).astype(jnp.float32)
    mean_sq = jnp.mean(raw_rows * raw_rows, axis=-1, keepdims=True)
    scaled = raw_rows * lax.rsqrt(4.0 * total_slots * (mean_sq + 1e-06))
    live = jnp.arange(block_count) < counts[0, 0]
    target = routes[0]
    own_blocks = compact(scaled, live & (target == my_time), slot_count)
    ahead_blocks = compact(scaled, live & (target == my_time + 1), slot_count)
    incoming, previous = passed_along((ahead_blocks, process), "tm", 1)
    gram_input = jnp.concatenate([own_blocks, incoming], axis=0).reshape(-1, order_size)
    shard_rows = lax.all_gather(gram_input, "swath", axis=0, tiled=True)
    columns = lax.dynamic_slice_in_dim(shard_rows, row_start, row_count, 1)
    gram = lax.dot_general(
        columns, shard_rows, (((0,), (0,)), ((), ())), preferred_element_type=jnp.float32
    )
    unit_rows = jnp.arange(order_size)[None, :] == jnp.arange(row_count)[:, None] + row_start
    diag_rows = previous[0].astype(jnp.float32) + process[0].astype(jnp.float32) + gram
    diag_rows = diag_rows + jnp.where(unit_rows, prior_prec[0][:, None], 0.0)
    coup_rows = -process[0].astype(jnp.float32)
    unit_full = jnp.eye(order_size, dtype=jnp.float32)
    for level in range(LEVELS):
        distance = 2**level
        full_diag, full_coup = (
            lax.all_gather(diag_rows, "swath", axis=0, tiled=True),
            lax.all_gather(coup_rows, "swath", axis=0, tiled=True),
        )
        factor = jnp.linalg.cholesky(full_diag)
        solved = tri_solve(factor, full_coup)
        own_cols = lax.dynamic_slice_in_dim(solved, row_start, row_count, 1)
        eliminated = inner_rows(own_cols, solved)
        left_term = passed_along(eliminated, "tm", distance)
        far_factor, far_solved = passed_along((factor, solved), "tm", -distance)
        has_partner = my_time + distance < time_count
        far_factor = jnp.where(has_partner, far_factor, unit_full)
        cross = tri_solve(far_factor, full_coup.T)
        cross_cols = lax.dynamic_slice_in_dim(cross, row_start, row_count, 1)
        right_term = inner_rows(cross_cols, cross)
        new_coupling = inner_rows(cross_cols, far_solved)
        diag_rows = diag_rows - left_term - jnp.where(has_partner, right_term, 0.0)
        coup_rows = -new_coupling
    return (diag_rows[None], coup_rows[None])


def solution(mesh):
    return jax.shard_map(
        shards,
        mesh=mesh,
        in_specs=(
            P("tm", "swath", None),
            P("tm", "swath", None),
            P("tm", "swath"),
            P("tm", "swath"),
            P("tm", "swath"),
        ),
        out_specs=(P("tm", "swath", None), P("tm", "swath", None)),
        check_vma=False,
    )
```

profile of v0, /device:TPU:16, one launch (start us, length us, event | category | flops | bytes accessed | tf_op | source)
XLA Modules:
  0.0 882.1 jit_solution(11233047935860242572)
XLA Ops:
  17.1 4.4 collective-permute-done.1
  24.6 4.3 collective-permute-done
  28.9 35.5 %all-gather.9.cloned.1.call-done = bf16[2048,512]{1,0:T(8,128)(2,1)} async-done(((bf16[512,512]{1,0:T(8,128)(2,1)}), bf16[2048,512]{1,0:T(8,128)(2,1)}) %all-gather.9.cloned.1.call-update) | async-done | bytes 2097168 | tf_op jit(solution)/shard_map/all_gather | solution.py:56
  64.4 3.3 fusion.71
  68.6 30.6 %all-gather.11.cloned.1.call-done = f32[512,512]{0,1:T(8,128)} async-done(((f32[128,512]{0,1:T(8,128)}), f32[512,512]{0,1:T(8,128)}) %all-gather.11.cloned.1.call-update) | async-done | bytes 1048592 | tf_op jit(solution)/shard_map/all_gather | solution.py:69
  101.1 11.7 %cholesky.374 = f32[128,128]{1,0:T(8,128)S(1)} custom-call(f32[128,128]{1,0:T(8,128)S(1)} %cholesky.586), custom_call_target="Cholesky" | custom-call | tf_op jit(solution)/shard_map/jit(cholesky)/cholesky | solution.py:72
  113.0 9.8 %custom-call.34 = f32[1,128,128]{1,2,0:T(8,128)S(1)} custom-call(f32[1,128,128]{2,1,0:T(8,128)S(1)} %get-tuple-element.152), custom_call_target="InvertDiagBlocksLowerTriangular" | custom-call | tf_op jit(solution)/shard_map/jit(cholesky)/cholesky | solution.py:72
  123.5 11.7 %cholesky.393 = f32[128,128]{1,0:T(8,128)S(1)} custom-call(f32[128,128]{1,0:T(8,128)S(1)} %cholesky.590), custom_call_target="Cholesky" | custom-call | tf_op jit(solution)/shard_map/jit(cholesky)/cholesky | solution.py:72
  135.2 10.2 %custom-call.35 = f32[1,128,128]{1,2,0:T(8,128)S(1)} custom-call(f32[1,128,128]{2,1,0:T(8,128)S(1)} %get-tuple-element.149), custom_call_target="InvertDiagBlocksLowerTriangular" | custom-call | tf_op jit(solution)/shard_map/jit(cholesky)/cholesky | solution.py:72
  146.1 11.7 %cholesky.414 = f32[128,128]{1,0:T(8,128)S(1)} custom-call(f32[128,128]{1,0:T(8,128)S(1)} %cholesky.595), custom_call_target="Cholesky" | custom-call | tf_op jit(solution)/shard_map/jit(cholesky)/cholesky | solution.py:72
  157.9 9.8 %custom-call.36 = f32[1,128,128]{1,2,0:T(8,128)S(1)} custom-call(f32[1,128,128]{2,1,0:T(8,128)S(1)} %get-tuple-element.146), custom_call_target="InvertDiagBlocksLowerTriangular" | custom-call | tf_op jit(solution)/shard_map/jit(cholesky)/cholesky | solution.py:72
  168.3 11.7 %cholesky.431 = f32[128,128]{1,0:T(8,128)S(1)} custom-call(f32[128,128]{1,0:T(8,128)S(1)} %convolution_subtract_fusion.14), custom_call_target="Cholesky" | custom-call | tf_op jit(solution)/shard_map/jit(cholesky)/cholesky | solution.py:72
  185.5 7.5 while.12
  193.0 39.3 %custom-call.37 = f32[4,128,128]{1,2,0:T(8,128)S(1)} custom-call(f32[4,128,128]{2,1,0:T(8,128)S(1)} %get-tuple-element.47), custom_call_target="InvertDiagBlocksLowerTriangular" | custom-call | tf_op jit(solution)/shard_map/triangular_solve/custom-call.3 | solution.py:16
  241.2 2.5 fusion.103
  243.7 2.4 collective-permute-start.2
  246.1 5.0 collective-permute-done.3
  251.9 10.2 %while.13 = (s32[]{:T(128)}, f32[512,512]{1,0:T(8,128)S(1)}, s32[4,2]{0,1:T(2,128)S(1)}, f32[4,128,128]{2,1,0:T(8,128)}, s32[]{:T(128)}) while((s32[]{:T(128)}, f32[512,512]{1,0:T(8,128)S(1)}, s32[4,2]{0,1:T(2,128)S(1)}, f32[4,128,128]{2,1,0:T(8,128)}, s32[]{:T(128)}) %tuple.157), condition=%wide.while_cond.clone, body=%wide.while_body.clone.sunk | while | flops 2 | bytes 132205 | solution.py:16
  252.6 1.9 bitcast_dynamic-update-slice_fusion.13
  262.2 40.7 %custom-call.38 = f32[4,128,128]{1,2,0:T(8,128)} custom-call(f32[4,128,128]{2,1,0:T(8,128)} %get-tuple-element.48), custom_call_target="InvertDiagBlocksLowerTriangular" | custom-call | tf_op jit(solution)/shard_map/triangular_solve/custom-call.3 | solution.py:16
  308.0 2.5 subtract_subtract_fusion.1
  310.6 3.8 collective-permute-start.4
  314.4 12.3 %collective-permute-done.4 = f32[512,512]{1,0:T(8,128)S(1)} collective-permute-done((f32[512,512]{1,0:T(8,128)S(1)}, f32[512,512]{1,0:T(8,128)S(1)}, u32[]{:S(2)}, u32[]{:S(2)}) %collective-permute-start.4) | collective-permute-done | bytes 1048608 | tf_op jit(solution)/shard_map/ppermute | solution.py:12
  328.6 15.1 %all-gather.13.cloned.1.call-done = f32[512,512]{0,1:T(8,128)} async-done(((f32[128,512]{0,1:T(8,128)}), f32[512,512]{0,1:T(8,128)}) %all-gather.13.cloned.1.call-update) | async-done | bytes 1048592 | tf_op jit(solution)/shard_map/all_gather | solution.py:69
  345.6 11.7 %cholesky.446 = f32[128,128]{1,0:T(8,128)S(1)} custom-call(f32[128,128]{1,0:T(8,128)S(1)} %cholesky.599), custom_call_target="Cholesky" | custom-call | tf_op jit(solution)/shard_map/jit(cholesky)/cholesky | solution.py:72
  357.5 9.8 %custom-call.39 = f32[1,128,128]{1,2,0:T(8,128)S(1)} custom-call(f32[1,128,128]{2,1,0:T(8,128)S(1)} %get-tuple-element.142), custom_call_target="InvertDiagBlocksLowerTriangular" | custom-call | tf_op jit(solution)/shard_map/jit(cholesky)/cholesky | solution.py:72
  368.0 11.7 %cholesky.465 = f32[128,128]{1,0:T(8,128)S(1)} custom-call(f32[128,128]{1,0:T(8,128)S(1)} %cholesky.603), custom_call_target="Cholesky" | custom-call | tf_op jit(solution)/shard_map/jit(cholesky)/cholesky | solution.py:72
  379.7 10.0 %custom-call.40 = f32[1,128,128]{1,2,0:T(8,128)S(1)} custom-call(f32[1,128,128]{2,1,0:T(8,128)S(1)} %get-tuple-element.139), custom_call_target="InvertDiagBlocksLowerTriangular" | custom-call | tf_op jit(solution)/shard_map/jit(cholesky)/cholesky | solution.py:72
  390.4 11.7 %cholesky.486 = f32[128,128]{1,0:T(8,128)S(1)} custom-call(f32[128,128]{1,0:T(8,128)S(1)} %cholesky.608), custom_call_target="Cholesky" | custom-call | tf_op jit(solution)/shard_map/jit(cholesky)/cholesky | solution.py:72
  402.1 9.8 %custom-call.41 = f32[1,128,128]{1,2,0:T(8,128)S(1)} custom-call(f32[1,128,128]{2,1,0:T(8,128)S(1)} %get-tuple-element.136), custom_call_target="InvertDiagBlocksLowerTriangular" | custom-call | tf_op jit(solution)/shard_map/jit(cholesky)/cholesky | solution.py:72
  412.5 11.7 %cholesky.503 = f32[128,128]{1,0:T(8,128)S(1)} custom-call(f32[128,128]{1,0:T(8,128)S(1)} %convolution_subtract_fusion.13), custom_call_target="Cholesky" | custom-call | tf_op jit(solution)/shard_map/jit(cholesky)/cholesky | solution.py:72
  429.7 7.5 while.14
  437.3 39.3 %custom-call.42 = f32[4,128,128]{1,2,0:T(8,128)S(1)} custom-call(f32[4,128,128]{2,1,0:T(8,128)S(1)} %get-tuple-element.49), custom_call_target="InvertDiagBlocksLowerTriangular" | custom-call | tf_op jit(solution)/shard_map/triangular_solve/custom-call.3 | solution.py:16
  480.3 2.4 collective-permute-start.6
  484.4 2.5 fusion.101
  486.9 3.8 collective-permute-start.5
  490.7 15.6 %collective-permute-done.6 = f32[512,512]{1,0:T(8,128)S(1)} collective-permute-done((f32[512,512]{1,0:T(8,128)S(1)}, f32[512,512]{1,0:T(8,128)S(1)}, u32[]{:S(2)}, u32[]{:S(2)}) %collective-permute-start.6) | collective-permute-done | bytes 1048608 | tf_op jit(solution)/shard_map/ppermute | solution.py:12
  507.1 10.2 %while.15 = (s32[]{:T(128)}, f32[512,512]{1,0:T(8,128)S(1)}, s32[4,2]{0,1:T(2,128)S(1)}, f32[4,128,128]{2,1,0:T(8,128)}, s32[]{:T(128)}) while((s32[]{:T(128)}, f32[512,512]{1,0:T(8,128)S(1)}, s32[4,2]{0,1:T(2,128)S(1)}, f32[4,128,128]{2,1,0:T(8,128)}, s32[]{:T(128)}) %tuple.159), condition=%wide.while_cond.clone.2, body=%wide.while_body.clone.2.sunk | while | flops 2 | bytes 132205 | solution.py:16
  512.8 1.9 bitcast_dynamic-update-slice_fusion.15
  517.3 40.7 %custom-call.43 = f32[4,128,128]{1,2,0:T(8,128)} custom-call(f32[4,128,128]{2,1,0:T(8,128)} %get-tuple-element.50), custom_call_target="InvertDiagBlocksLowerTriangular" | custom-call | tf_op jit(solution)/shard_map/triangular_solve/custom-call.3 | solution.py:16
  564.8 2.5 subtract_subtract_fusion
  567.4 2.6 collective-permute-start.7
  570.0 23.3 %collective-permute-done.7 = f32[512,512]{1,0:T(8,128)S(1)} collective-permute-done((f32[512,512]{1,0:T(8,128)S(1)}, f32[512,512]{1,0:T(8,128)S(1)}, u32[]{:S(2)}, u32[]{:S(2)}) %collective-permute-start.7) | collective-permute-done | bytes 1048608 | tf_op jit(solution)/shard_map/ppermute | solution.py:12
  594.9 4.9 all-gather.17.cloned.1.call-done
  601.6 11.7 %cholesky.518 = f32[128,128]{1,0:T(8,128)S(1)} custom-call(f32[128,128]{1,0:T(8,128)S(1)} %cholesky.612), custom_call_target="Cholesky" | custom-call | tf_op jit(solution)/shard_map/jit(cholesky)/cholesky | solution.py:72
  613.5 9.8 %custom-call.44 = f32[1,128,128]{1,2,0:T(8,128)S(1)} custom-call(f32[1,128,128]{2,1,0:T(8,128)S(1)} %get-tuple-element.132), custom_call_target="InvertDiagBlocksLowerTriangular" | custom-call | tf_op jit(solution)/shard_map/jit(cholesky)/cholesky | solution.py:72
  624.0 11.7 %cholesky.537 = f32[128,128]{1,0:T(8,128)S(1)} custom-call(f32[128,128]{1,0:T(8,128)S(1)} %cholesky.616), custom_call_target="Cholesky" | custom-call | tf_op jit(solution)/shard_map/jit(cholesky)/cholesky | solution.py:72
  635.8 10.0 %custom-call.45 = f32[1,128,128]{1,2,0:T(8,128)S(1)} custom-call(f32[1,128,128]{2,1,0:T(8,128)S(1)} %get-tuple-element.129), custom_call_target="InvertDiagBlocksLowerTriangular" | custom-call | tf_op jit(solution)/shard_map/jit(cholesky)/cholesky | solution.py:72
  646.4 11.7 %cholesky.558 = f32[128,128]{1,0:T(8,128)S(1)} custom-call(f32[128,128]{1,0:T(8,128)S(1)} %cholesky.621), custom_call_target="Cholesky" | custom-call | tf_op jit(solution)/shard_map/jit(cholesky)/cholesky | solution.py:72
  658.2 9.8 %custom-call.46 = f32[1,128,128]{1,2,0:T(8,128)S(1)} custom-call(f32[1,128,128]{2,1,0:T(8,128)S(1)} %get-tuple-element.126), custom_call_target="InvertDiagBlocksLowerTriangular" | custom-call | tf_op jit(solution)/shard_map/jit(cholesky)/cholesky | solution.py:72
  668.6 12.1 %cholesky.575 = f32[128,128]{1,0:T(8,128)S(1)} custom-call(f32[128,128]{1,0:T(8,128)S(1)} %convolution_subtract_fusion.12), custom_call_target="Cholesky" | custom-call | tf_op jit(solution)/shard_map/jit(cholesky)/cholesky | solution.py:72
  686.0 7.9 while.16
  693.9 39.3 %custom-call.47 = f32[4,128,128]{1,2,0:T(8,128)S(1)} custom-call(f32[4,128,128]{2,1,0:T(8,128)S(1)} %get-tuple-element.51), custom_call_target="InvertDiagBlocksLowerTriangular" | custom-call | tf_op jit(solution)/shard_map/triangular_solve/custom-call.3 | solution.py:16
  736.9 2.4 collective-permute-start.9
  742.9 2.5 fusion.99
  745.4 6.2 collective-permute-start.8
  751.6 59.3 %collective-permute-done.9 = f32[512,512]{1,0:T(8,128)S(1)} collective-permute-done((f32[512,512]{1,0:T(8,128)S(1)}, f32[512,512]{1,0:T(8,128)S(1)}, u32[]{:S(2)}, u32[]{:S(2)}) %collective-permute-start.9) | collective-permute-done | bytes 1048608 | tf_op jit(solution)/shard_map/ppermute | solution.py:12
  811.8 10.4 %while.17 = (s32[]{:T(128)}, f32[512,512]{1,0:T(8,128)S(1)}, s32[4,2]{0,1:T(2,128)S(1)}, f32[4,128,128]{2,1,0:T(8,128)}, s32[]{:T(128)}) while((s32[]{:T(128)}, f32[512,512]{1,0:T(8,128)S(1)}, s32[4,2]{0,1:T(2,128)S(1)}, f32[4,128,128]{2,1,0:T(8,128)}, s32[]{:T(128)}) %tuple.161), condition=%wide.while_cond.clone.4, body=%wide.while_body.clone.4.sunk | while | flops 2 | bytes 132205 | solution.py:16
  812.4 2.0 bitcast_dynamic-update-slice_fusion.17
  815.0 2.0 bitcast_dynamic-update-slice_fusion.17
  817.6 2.0 bitcast_dynamic-update-slice_fusion.17
  820.2 2.0 bitcast_dynamic-update-slice_fusion.17
  822.2 40.7 %custom-call.48 = f32[4,128,128]{1,2,0:T(8,128)} custom-call(f32[4,128,128]{2,1,0:T(8,128)} %get-tuple-element.52), custom_call_target="InvertDiagBlocksLowerTriangular" | custom-call | tf_op jit(solution)/shard_map/triangular_solve/custom-call.3 | solution.py:16
  872.3 2.7 fusion
  (268 shorter events, 123.9 us)
Async XLA Ops:
  7.2 57.3 %all-gather.9.cloned.1.call-start = ((), (), s32[]{:S(2)}) async-start(), calls=%async_computation | async-start | bytes 2621440 | tf_op jit(solution)/shard_map/all_gather | solution.py:56
  13.1 9.3 %copy-start.12 = (bf16[1,128,512]{2,1,0:T(8,128)(2,1)S(1)}, bf16[1,128,512]{2,1,0:T(8,128)(2,1)}, u32[]{:S(2)}) copy-start(bf16[1,128,512]{2,1,0:T(8,128)(2,1)} %param.11) | copy-start | bytes 393220
  13.7 50.7 %copy-start.13 = (f32[1,128]{1,0:T(1,128)S(1)}, f32[1,128]{1,0:T(1,128)}, u32[]{:S(2)}) copy-start(f32[1,128]{1,0:T(1,128)} %param.12) | copy-start | bytes 1540
  13.9 7.7 collective-permute-start.1
  22.4 76.8 %all-gather.11.cloned.1.call-start = ((), (), s32[]{:S(2)}) async-start(), calls=%async_computation.1 | async-start | bytes 1310720 | tf_op jit(solution)/shard_map/all_gather | solution.py:69
  22.6 6.3 collective-permute-start
  67.8 164.6 %all-gather.21.cloned.1.call-start = ((), (), s32[]{:S(2)}) async-start(), calls=%async_computation.6 | async-start | bytes 1310720 | tf_op jit(solution)/shard_map/all_gather | solution.py:70
  68.6 275.1 %all-gather.13.cloned.1.call-start = ((), (), s32[]{:S(2)}) async-start(), calls=%async_computation.2 | async-start | bytes 1310720 | tf_op jit(solution)/shard_map/all_gather | solution.py:69
  99.2 1.7 copy-start.4
  232.4 3.5 copy-start.5
  236.9 14.2 %collective-permute-start.3 = (f32[512,512]{1,0:T(8,128)S(1)}, f32[512,512]{1,0:T(8,128)S(1)}, u32[]{:S(2)}, u32[]{:S(2)}) collective-permute-start(f32[512,512]{1,0:T(8,128)S(1)} %get-tuple-element.110), channel_id=1, source_target_pairs={{4,0},{8,4},{12,8},{16,12},{20,16},{24,20},{28,24},{32,28},{36,32}... | collective-permute-start | bytes 3145736 | tf_op jit(solution)/shard_map/ppermute | solution.py:12
  243.7 64.2 %collective-permute-start.2 = (f32[128,512]{0,1:T(8,128)}, f32[128,512]{0,1:T(8,128)S(1)}, u32[]{:S(2)}, u32[]{:S(2)}) collective-permute-start(f32[128,512]{0,1:T(8,128)} %fusion.103), channel_id=1, source_target_pairs={{0,4},{4,8},{8,12},{12,16},{16,20},{20,24},{24,28},{28,32},{32,36}... | collective-permute-start | bytes 786440 | tf_op jit(solution)/shard_map/ppermute | solution.py:12
  302.9 3.4 copy-start.9
  306.8 1.2 copy-start.8
  310.5 166.1 %all-gather.15.cloned.1.call-start = ((), (), s32[]{:S(2)}) async-start(), calls=%async_computation.3 | async-start | bytes 1310720 | tf_op jit(solution)/shard_map/all_gather | solution.py:70
  310.6 16.1 %collective-permute-start.4 = (f32[512,512]{1,0:T(8,128)S(1)}, f32[512,512]{1,0:T(8,128)S(1)}, u32[]{:S(2)}, u32[]{:S(2)}) collective-permute-start(f32[512,512]{1,0:T(8,128)S(1)} %pad_maximum_fusion), channel_id=1, source_target_pairs={{4,0},{8,4},{12,8},{16,12},{20,16},{24,20},{28,24},{32,28},{36,32}... | collective-permute-start | bytes 3145736 | tf_op jit(solution)/shard_map/ppermute | solution.py:12
  328.2 271.6 %all-gather.17.cloned.1.call-start = ((), (), s32[]{:S(2)}) async-start(), calls=%async_computation.4 | async-start | bytes 1310720 | tf_op jit(solution)/shard_map/all_gather | solution.py:69
  343.7 1.7 copy-start.2
  476.6 6.1 copy-start.1
  480.3 25.9 %collective-permute-start.6 = (f32[512,512]{1,0:T(8,128)S(1)}, f32[512,512]{1,0:T(8,128)S(1)}, u32[]{:S(2)}, u32[]{:S(2)}) collective-permute-start(f32[512,512]{1,0:T(8,128)S(1)} %get-tuple-element.108), channel_id=1, source_target_pairs={{8,0},{12,4},{16,8},{20,12},{24,16},{28,20},{32,24},{36,28},{40,32... | collective-permute-start | bytes 3145736 | tf_op jit(solution)/shard_map/ppermute | solution.py:12
  486.9 77.9 %collective-permute-start.5 = (f32[128,512]{0,1:T(8,128)}, f32[128,512]{0,1:T(8,128)S(1)}, u32[]{:S(2)}, u32[]{:S(2)}) collective-permute-start(f32[128,512]{0,1:T(8,128)} %fusion.101), channel_id=1, source_target_pairs={{0,8},{4,12},{8,16},{12,20},{16,24},{20,28},{24,32},{28,36},{32,40... | collective-permute-start | bytes 786440 | tf_op jit(solution)/shard_map/ppermute | solution.py:12
  558.1 4.2 copy-start.10
  562.7 2.0 copy-start.7
  567.3 165.9 %all-gather.19.cloned.1.call-start = ((), (), s32[]{:S(2)}) async-start(), calls=%async_computation.5 | async-start | bytes 1310720 | tf_op jit(solution)/shard_map/all_gather | solution.py:70
  567.4 26.0 %collective-permute-start.7 = (f32[512,512]{1,0:T(8,128)S(1)}, f32[512,512]{1,0:T(8,128)S(1)}, u32[]{:S(2)}, u32[]{:S(2)}) collective-permute-start(f32[512,512]{1,0:T(8,128)S(1)} %pad_maximum_fusion.2), channel_id=1, source_target_pairs={{8,0},{12,4},{16,8},{20,12},{24,16},{28,20},{32,24},{36,28},{40,32... | collective-permute-start | bytes 3145736 | tf_op jit(solution)/shard_map/ppermute | solution.py:12
  599.7 1.7 copy-start.3
  733.2 6.1 copy-start
  736.9 74.0 %collective-permute-start.9 = (f32[512,512]{1,0:T(8,128)S(1)}, f32[512,512]{1,0:T(8,128)S(1)}, u32[]{:S(2)}, u32[]{:S(2)}) collective-permute-start(f32[512,512]{1,0:T(8,128)S(1)} %get-tuple-element.106), channel_id=1, source_target_pairs={{16,0},{20,4},{24,8},{28,12},{32,16},{36,20},{40,24},{44,28},{48,3... | collective-permute-start | bytes 3145736 | tf_op jit(solution)/shard_map/ppermute | solution.py:12
  740.9 131.4 %collective-permute-start.10 = (f32[512,512]{1,0:T(8,128)S(1)}, f32[512,512]{1,0:T(8,128)}, u32[]{:S(2)}, u32[]{:S(2)}) collective-permute-start(f32[512,512]{1,0:T(8,128)S(1)} %pad_maximum_fusion.4), channel_id=1, source_target_pairs={{16,0},{20,4},{24,8},{28,12},{32,16},{36,20},{40,24},{44,28},{48,3... | collective-permute-start | bytes 3145736 | tf_op jit(solution)/shard_map/ppermute | solution.py:12
  745.4 124.3 %collective-permute-start.8 = (f32[128,512]{0,1:T(8,128)}, f32[128,512]{0,1:T(8,128)S(1)}, u32[]{:S(2)}, u32[]{:S(2)}) collective-permute-start(f32[128,512]{0,1:T(8,128)} %fusion.99), channel_id=1, source_target_pairs={{0,16},{4,20},{8,24},{12,28},{16,32},{20,36},{24,40},{28,44},{32,4... | collective-permute-start | bytes 786440 | tf_op jit(solution)/shard_map/ppermute | solution.py:12
  862.9 4.2 copy-start.11
  867.6 2.0 copy-start.6
Sparse Core Ops, SparseCore 0:
  22.5 41.8 all-gather.8
  67.9 31.2 all-gather.10
  101.9 32.4 all-gather.20
  310.6 33.0 all-gather.12
  346.2 30.5 all-gather.14
  567.5 32.2 all-gather.16
  602.4 30.6 all-gather.18
where the time goes:
time: 894 us; the launch traced here: 882 us
  other arithmetic  487 us (54%)
  waiting for transfers between devices  210 us (23%)
  local copies, waits for them, and re-layouts  64.4 us (7%)
  matrix products  64 us (7%)
  starting transfers between devices  32.1 us (4%)
  between operations  23.4 us (3%)
    another operation x19, other arithmetic, tri_solve(): lax.linalg.triangular_solve(factor, right, left_side=True, lower=True)  242 us
    another operation x45, other arithmetic, shards(): factor = jnp.linalg.cholesky(full_diag)  238 us
    ppermute x11, waiting for transfers between devices, passed_along(): return lax.ppermute(block, axis, route)  124 us
    another operation x79, local copies, waits for them, and re-layouts, tri_solve(): lax.linalg.triangular_solve(factor, right, left_side=True, lower=True)  55.7 us
    all_gather x3, waiting for transfers between devices, shards(): lax.all_gather(diag_rows, 'swath', axis=0, tiled=True)  50.5 us
    all_gather x1, waiting for transfers between devices, shards(): shard_rows = lax.all_gather(gram_input, 'swath', axis=0, tiled=True)  35.5 us
    another operation x42, matrix products, tri_solve(): lax.linalg.triangular_solve(factor, right, left_side=True, lower=True)  35 us
    ppermute x11, starting transfers between devices, passed_along(): return lax.ppermute(block, axis, route)  31.4 us
  transfers between devices with their start and end apart: 18, of which 11 were waited for; matrix products, arithmetic and copies ran while one was open for 66% of the time, Pallas kernels for 0%

commit v1 on v0

--- a/solution.py
+++ b/solution.py
@@ -66,7 +66,10 @@
     for level in range(LEVELS):
         distance = 2**level
         full_diag, full_coup = (
-            lax.all_gather(diag_rows, "swath", axis=0, tiled=True),
+            jnp.concatenate(
+                lax.all_to_all(jnp.stack([diag_rows] * lax.axis_size("swath")), "swath", 0, 0),
+                axis=0,
+            ),
             lax.all_gather(coup_rows, "swath", axis=0, tiled=True),
         )
         factor = jnp.linalg.cholesky(full_diag)

time: 894 us -> 820 us (0.917)
  the two profiles are of different devices: /device:TPU:16 before, /device:TPU:57 now
where the time goes in v1:
time: 820 us; the launch traced here: 809 us
  other arithmetic  490 us (60%)
  waiting for transfers between devices  124 us (15%)
  local copies, waits for them, and re-layouts  59 us (7%)
  matrix products  57.8 us (7%)
  starting transfers between devices  53.5 us (7%)
  between operations  23.5 us (3%)
    another operation x19, other arithmetic, tri_solve(): lax.linalg.triangular_solve(factor, right, left_side=True, lower=True)  244 us
    another operation x45, other arithmetic, shards(): factor = jnp.linalg.cholesky(full_diag)  239 us
    ppermute x11, waiting for transfers between devices, passed_along(): return lax.ppermute(block, axis, route)  54.9 us
    another operation x79, local copies, waits for them, and re-layouts, tri_solve(): lax.linalg.triangular_solve(factor, right, left_side=True, lower=True)  51 us
    ppermute x11, starting transfers between devices, passed_along(): return lax.ppermute(block, axis, route)  42.2 us
    all_to_all x3, waiting for transfers between devices, shards(): lax.all_to_all(jnp.stack([diag_rows] * lax.axis_size('swath')), 'swath',...  35.6 us
    another operation x42, matrix products, tri_solve(): lax.linalg.triangular_solve(factor, right, left_side=True, lower=True)  34.1 us
    all_gather x1, waiting for transfers between devices, shards(): shard_rows = lax.all_gather(gram_input, 'swath', axis=0, tiled=True)  33.7 us
  transfers between devices with their start and end apart: 18, of which 10 were waited for; matrix products, arithmetic and copies ran while one was open for 72% of the time, Pallas kernels for 0%

profile of v1, /device:TPU:57, one launch (start us, length us, event | category | flops | bytes accessed | tf_op | source)
XLA Modules:
  0.0 808.5 jit_solution(2160679278824384987)
XLA Ops:
  13.9 3.8 collective-permute-start.1
  19.0 1.9 collective-permute-done.1
  21.8 6.5 collective-permute-start
  28.3 1.9 collective-permute-done
  30.2 33.7 %all-gather.6.cloned.1.call-done = bf16[2048,512]{1,0:T(8,128)(2,1)} async-done(((bf16[512,512]{1,0:T(8,128)(2,1)}), bf16[2048,512]{1,0:T(8,128)(2,1)}) %all-gather.6.cloned.1.call-update) | async-done | bytes 2097168 | tf_op jit(solution)/shard_map/all_gather | solution.py:56
  64.0 2.3 fusion.71
  67.5 3.5 all-to-all-start
  71.8 13.6 %all-to-all-done = f32[4,128,512]{1,2,0:T(8,128)S(1)} async-done(((f32[4,128,512]{1,2,0:T(8,128)}), f32[4,128,512]{1,2,0:T(8,128)S(1)}, u32[]{:S(2)}, u32[]{:S(2)}) %all-to-all-start) | async-done | bytes 1048608 | tf_op jit(solution)/shard_map/all_to_all | solution.py:70
  86.1 11.7 %cholesky.374 = f32[128,128]{1,0:T(8,128)S(1)} custom-call(f32[128,128]{1,0:T(8,128)S(1)} %cholesky.586), custom_call_target="Cholesky" | custom-call | tf_op jit(solution)/shard_map/jit(cholesky)/cholesky | solution.py:75
  98.0 9.8 %custom-call.34 = f32[1,128,128]{1,2,0:T(8,128)S(1)} custom-call(f32[1,128,128]{2,1,0:T(8,128)S(1)} %get-tuple-element.148), custom_call_target="InvertDiagBlocksLowerTriangular" | custom-call | tf_op jit(solution)/shard_map/jit(cholesky)/cholesky | solution.py:75
  108.5 11.7 %cholesky.393 = f32[128,128]{1,0:T(8,128)S(1)} custom-call(f32[128,128]{1,0:T(8,128)S(1)} %cholesky.590), custom_call_target="Cholesky" | custom-call | tf_op jit(solution)/shard_map/jit(cholesky)/cholesky | solution.py:75
  120.2 10.2 %custom-call.35 = f32[1,128,128]{1,2,0:T(8,128)S(1)} custom-call(f32[1,128,128]{2,1,0:T(8,128)S(1)} %get-tuple-element.145), custom_call_target="InvertDiagBlocksLowerTriangular" | custom-call | tf_op jit(solution)/shard_map/jit(cholesky)/cholesky | solution.py:75
  131.2 11.7 %cholesky.414 = f32[128,128]{1,0:T(8,128)S(1)} custom-call(f32[128,128]{1,0:T(8,128)S(1)} %cholesky.595), custom_call_target="Cholesky" | custom-call | tf_op jit(solution)/shard_map/jit(cholesky)/cholesky | solution.py:75
  142.9 9.8 %custom-call.36 = f32[1,128,128]{1,2,0:T(8,128)S(1)} custom-call(f32[1,128,128]{2,1,0:T(8,128)S(1)} %get-tuple-element.142), custom_call_target="InvertDiagBlocksLowerTriangular" | custom-call | tf_op jit(solution)/shard_map/jit(cholesky)/cholesky | solution.py:75
  153.3 11.7 %cholesky.431 = f32[128,128]{1,0:T(8,128)S(1)} custom-call(f32[128,128]{1,0:T(8,128)S(1)} %convolution_subtract_fusion.14), custom_call_target="Cholesky" | custom-call | tf_op jit(solution)/shard_map/jit(cholesky)/cholesky | solution.py:75
  170.8 8.1 %while.12 = (s32[]{:T(128)}, f32[512,512]{1,0:T(8,128)S(1)}, s32[4,2]{0,1:T(2,128)S(1)}, f32[4,128,128]{2,1,0:T(8,128)S(1)}, s32[]{:T(128)}) while((s32[]{:T(128)}, f32[512,512]{1,0:T(8,128)S(1)}, s32[4,2]{0,1:T(2,128)S(1)}, f32[4,128,128]{2,1,0:T(8,128)S(1)}, s32[]{:T(128)}) %tuple.123), condition=%wide.while_cond, body=%wide.while_body.sunk | while | flops 2 | bytes 131189 | solution.py:16
  178.9 39.9 %custom-call.37 = f32[4,128,128]{1,2,0:T(8,128)} custom-call(f32[4,128,128]{2,1,0:T(8,128)S(1)} %get-tuple-element.47), custom_call_target="InvertDiagBlocksLowerTriangular" | custom-call | tf_op jit(solution)/shard_map/triangular_solve/custom-call.3 | solution.py:16
  223.4 3.4 collective-permute-start.3
  228.5 1.9 collective-permute-start.4
  231.9 5.7 collective-permute-start.2
  237.7 4.0 collective-permute-done.3
  242.5 10.4 %while.13 = (s32[]{:T(128)}, f32[512,512]{1,0:T(8,128)S(1)}, s32[4,2]{0,1:T(2,128)S(1)}, f32[4,128,128]{2,1,0:T(8,128)}, s32[]{:T(128)}) while((s32[]{:T(128)}, f32[512,512]{1,0:T(8,128)S(1)}, s32[4,2]{0,1:T(2,128)S(1)}, f32[4,128,128]{2,1,0:T(8,128)}, s32[]{:T(128)}) %tuple.149), condition=%wide.while_cond.clone, body=%wide.while_body.clone.sunk | while | flops 2 | bytes 132205 | solution.py:16
  243.1 2.0 bitcast_dynamic-update-slice_fusion.13
  245.7 2.0 bitcast_dynamic-update-slice_fusion.13
  248.4 2.0 bitcast_dynamic-update-slice_fusion.13
  251.0 2.0 bitcast_dynamic-update-slice_fusion.13
  252.9 40.7 %custom-call.38 = f32[4,128,128]{1,2,0:T(8,128)} custom-call(f32[4,128,128]{2,1,0:T(8,128)} %get-tuple-element.48), custom_call_target="InvertDiagBlocksLowerTriangular" | custom-call | tf_op jit(solution)/shard_map/triangular_solve/custom-call.3 | solution.py:16
  303.4 3.5 all-to-all-start.1
  307.4 2.7 convolution_negate_fusion.2
  310.1 10.1 %all-to-all-done.1 = f32[4,128,512]{1,2,0:T(8,128)S(1)} async-done(((f32[4,128,512]{1,2,0:T(8,128)}), f32[4,128,512]{1,2,0:T(8,128)S(1)}, u32[]{:S(2)}, u32[]{:S(2)}) %all-to-all-start.1) | async-done | bytes 1048608 | tf_op jit(solution)/shard_map/all_to_all | solution.py:70
  320.9 11.7 %cholesky.446 = f32[128,128]{1,0:T(8,128)S(1)} custom-call(f32[128,128]{1,0:T(8,128)S(1)} %cholesky.599), custom_call_target="Cholesky" | custom-call | tf_op jit(solution)/shard_map/jit(cholesky)/cholesky | solution.py:75
  332.8 9.8 %custom-call.39 = f32[1,128,128]{1,2,0:T(8,128)S(1)} custom-call(f32[1,128,128]{2,1,0:T(8,128)S(1)} %get-tuple-element.138), custom_call_target="InvertDiagBlocksLowerTriangular" | custom-call | tf_op jit(solution)/shard_map/jit(cholesky)/cholesky | solution.py:75
  343.2 11.7 %cholesky.465 = f32[128,128]{1,0:T(8,128)S(1)} custom-call(f32[128,128]{1,0:T(8,128)S(1)} %cholesky.603), custom_call_target="Cholesky" | custom-call | tf_op jit(solution)/shard_map/jit(cholesky)/cholesky | solution.py:75
  355.0 10.0 %custom-call.40 = f32[1,128,128]{1,2,0:T(8,128)S(1)} custom-call(f32[1,128,128]{2,1,0:T(8,128)S(1)} %get-tuple-element.135), custom_call_target="InvertDiagBlocksLowerTriangular" | custom-call | tf_op jit(solution)/shard_map/jit(cholesky)/cholesky | solution.py:75
  365.6 11.7 %cholesky.486 = f32[128,128]{1,0:T(8,128)S(1)} custom-call(f32[128,128]{1,0:T(8,128)S(1)} %cholesky.608), custom_call_target="Cholesky" | custom-call | tf_op jit(solution)/shard_map/jit(cholesky)/cholesky | solution.py:75
  377.4 9.8 %custom-call.41 = f32[1,128,128]{1,2,0:T(8,128)S(1)} custom-call(f32[1,128,128]{2,1,0:T(8,128)S(1)} %get-tuple-element.132), custom_call_target="InvertDiagBlocksLowerTriangular" | custom-call | tf_op jit(solution)/shard_map/jit(cholesky)/cholesky | solution.py:75
  387.8 12.1 %cholesky.503 = f32[128,128]{1,0:T(8,128)S(1)} custom-call(f32[128,128]{1,0:T(8,128)S(1)} %convolution_subtract_fusion.13), custom_call_target="Cholesky" | custom-call | tf_op jit(solution)/shard_map/jit(cholesky)/cholesky | solution.py:75
  406.5 7.9 while.14
  414.3 39.3 %custom-call.42 = f32[4,128,128]{1,2,0:T(8,128)S(1)} custom-call(f32[4,128,128]{2,1,0:T(8,128)S(1)} %get-tuple-element.49), custom_call_target="InvertDiagBlocksLowerTriangular" | custom-call | tf_op jit(solution)/shard_map/triangular_solve/custom-call.3 | solution.py:16
  453.7 3.1 collective-permute-start.6
  462.1 3.1 collective-permute-start.7
  466.7 4.3 collective-permute-start.5
  471.0 12.1 %collective-permute-done.6 = f32[512,512]{1,0:T(8,128)} collective-permute-done((f32[512,512]{1,0:T(8,128)}, f32[512,512]{1,0:T(8,128)}, u32[]{:S(2)}, u32[]{:S(2)}) %collective-permute-start.6) | collective-permute-done | bytes 1048608 | tf_op jit(solution)/shard_map/ppermute | solution.py:12
  484.5 8.1 %while.15 = (s32[]{:T(128)}, f32[512,512]{1,0:T(8,128)S(1)}, s32[4,2]{0,1:T(2,128)S(1)}, f32[4,128,128]{2,1,0:T(8,128)S(1)}, s32[]{:T(128)}) while((s32[]{:T(128)}, f32[512,512]{1,0:T(8,128)S(1)}, s32[4,2]{0,1:T(2,128)S(1)}, f32[4,128,128]{2,1,0:T(8,128)S(1)}, s32[]{:T(128)}) %tuple.151), condition=%wide.while_cond.clone.2, body=%wide.while_body.clone.2.sunk | while | flops 2 | bytes 131189 | solution.py:16
  492.7 39.9 %custom-call.43 = f32[4,128,128]{1,2,0:T(8,128)} custom-call(f32[4,128,128]{2,1,0:T(8,128)S(1)} %get-tuple-element.50), custom_call_target="InvertDiagBlocksLowerTriangular" | custom-call | tf_op jit(solution)/shard_map/triangular_solve/custom-call.3 | solution.py:16
  542.3 3.5 all-to-all-start.2
  546.1 2.7 convolution_negate_fusion.1
  548.9 11.9 %all-to-all-done.2 = f32[4,128,512]{1,2,0:T(8,128)S(1)} async-done(((f32[4,128,512]{1,2,0:T(8,128)}), f32[4,128,512]{1,2,0:T(8,128)S(1)}, u32[]{:S(2)}, u32[]{:S(2)}) %all-to-all-start.2) | async-done | bytes 1048608 | tf_op jit(solution)/shard_map/all_to_all | solution.py:70
  561.4 11.7 %cholesky.518 = f32[128,128]{1,0:T(8,128)S(1)} custom-call(f32[128,128]{1,0:T(8,128)S(1)} %cholesky.612), custom_call_target="Cholesky" | custom-call | tf_op jit(solution)/shard_map/jit(cholesky)/cholesky | solution.py:75
  573.3 9.8 %custom-call.44 = f32[1,128,128]{1,2,0:T(8,128)S(1)} custom-call(f32[1,128,128]{2,1,0:T(8,128)S(1)} %get-tuple-element.128), custom_call_target="InvertDiagBlocksLowerTriangular" | custom-call | tf_op jit(solution)/shard_map/jit(cholesky)/cholesky | solution.py:75
  583.7 11.7 %cholesky.537 = f32[128,128]{1,0:T(8,128)S(1)} custom-call(f32[128,128]{1,0:T(8,128)S(1)} %cholesky.616), custom_call_target="Cholesky" | custom-call | tf_op jit(solution)/shard_map/jit(cholesky)/cholesky | solution.py:75
  595.5 10.0 %custom-call.45 = f32[1,128,128]{1,2,0:T(8,128)S(1)} custom-call(f32[1,128,128]{2,1,0:T(8,128)S(1)} %get-tuple-element.125), custom_call_target="InvertDiagBlocksLowerTriangular" | custom-call | tf_op jit(solution)/shard_map/jit(cholesky)/cholesky | solution.py:75
  606.2 11.7 %cholesky.558 = f32[128,128]{1,0:T(8,128)S(1)} custom-call(f32[128,128]{1,0:T(8,128)S(1)} %cholesky.621), custom_call_target="Cholesky" | custom-call | tf_op jit(solution)/shard_map/jit(cholesky)/cholesky | solution.py:75
  617.9 9.8 %custom-call.46 = f32[1,128,128]{1,2,0:T(8,128)S(1)} custom-call(f32[1,128,128]{2,1,0:T(8,128)S(1)} %get-tuple-element.122), custom_call_target="InvertDiagBlocksLowerTriangular" | custom-call | tf_op jit(solution)/shard_map/jit(cholesky)/cholesky | solution.py:75
  628.3 12.1 %cholesky.575 = f32[128,128]{1,0:T(8,128)S(1)} custom-call(f32[128,128]{1,0:T(8,128)S(1)} %convolution_subtract_fusion.12), custom_call_target="Cholesky" | custom-call | tf_op jit(solution)/shard_map/jit(cholesky)/cholesky | solution.py:75
  647.0 1.9 collective-permute-start.9
  648.9 8.0 while.16
  656.9 39.9 %custom-call.47 = f32[4,128,128]{1,2,0:T(8,128)} custom-call(f32[4,128,128]{2,1,0:T(8,128)S(1)} %get-tuple-element.51), custom_call_target="InvertDiagBlocksLowerTriangular" | custom-call | tf_op jit(solution)/shard_map/triangular_solve/custom-call.3 | solution.py:16
  697.0 8.1 %while.17 = (s32[]{:T(128)}, f32[512,512]{1,0:T(8,128)S(1)}, s32[4,2]{0,1:T(2,128)S(1)}, f32[4,128,128]{2,1,0:T(8,128)S(1)}, s32[]{:T(128)}) while((s32[]{:T(128)}, f32[512,512]{1,0:T(8,128)S(1)}, s32[4,2]{0,1:T(2,128)S(1)}, f32[4,128,128]{2,1,0:T(8,128)S(1)}, s32[]{:T(128)}) %tuple.153), condition=%wide.while_cond.clone.4, body=%wide.while_body.clone.4.sunk | while | flops 2 | bytes 131189 | solution.py:16
  705.1 39.3 %custom-call.48 = f32[4,128,128]{1,2,0:T(8,128)S(1)} custom-call(f32[4,128,128]{2,1,0:T(8,128)S(1)} %get-tuple-element.52), custom_call_target="InvertDiagBlocksLowerTriangular" | custom-call | tf_op jit(solution)/shard_map/triangular_solve/custom-call.3 | solution.py:16
  750.6 3.1 collective-permute-start.10
  753.7 5.3 collective-permute-start.8
  764.0 5.2 collective-permute-done.8
  770.6 29.7 %collective-permute-done.10 = f32[512,512]{1,0:T(8,128)S(1)} collective-permute-done((f32[512,512]{1,0:T(8,128)S(1)}, f32[512,512]{1,0:T(8,128)S(1)}, u32[]{:S(2)}, u32[]{:S(2)}) %collective-permute-start.10) | collective-permute-done | bytes 1048608 | tf_op jit(solution)/shard_map/ppermute | solution.py:12
  (266 shorter events, 122.4 us)
Async XLA Ops:
  7.2 56.8 %all-gather.6.cloned.1.call-start = ((), (), s32[]{:S(2)}) async-start(), calls=%async_computation.3 | async-start | bytes 2621440 | tf_op jit(solution)/shard_map/all_gather | solution.py:56
  13.1 8.7 %copy-start.5 = (bf16[1,128,512]{2,1,0:T(8,128)(2,1)S(1)}, bf16[1,128,512]{2,1,0:T(8,128)(2,1)}, u32[]{:S(2)}) copy-start(bf16[1,128,512]{2,1,0:T(8,128)(2,1)} %param.11) | copy-start | bytes 393220
  13.2 50.8 %copy-start.10 = (f32[1,128]{1,0:T(1,128)S(1)}, f32[1,128]{1,0:T(1,128)}, u32[]{:S(2)}) copy-start(f32[1,128]{1,0:T(1,128)} %param.12) | copy-start | bytes 1540
  13.9 7.1 collective-permute-start.1
  21.8 8.4 %collective-permute-start = (bf16[1,128,512]{2,1,0:T(8,128)(2,1)S(1)}, bf16[1,128,512]{2,1,0:T(8,128)(2,1)S(1)}, u32[]{:S(2)}, u32[]{:S(2)}) collective-permute-start(bf16[1,128,512]{2,1,0:T(8,128)(2,1)S(1)} %copy-done.5), channel_id=1, source_target_pairs={{0,4},{4,8},{8,12},{12,16},{16,20},{20,24},{24,28},{28,32},{32,36}... | collective-permute-start | bytes 393224 | tf_op jit(solution)/shard_map/ppermute | solution.py:12
  67.5 18.0 %all-to-all-start = ((f32[4,128,512]{1,2,0:T(8,128)}), f32[4,128,512]{1,2,0:T(8,128)S(1)}, u32[]{:S(2)}, u32[]{:S(2)}) async-start(f32[4,128,512]{1,2,0:T(8,128)} %stack.6), calls=%async_computation | async-start | bytes 2097152 | tf_op jit(solution)/shard_map/all_to_all | solution.py:70
  71.0 147.9 %all-gather.12.cloned.1.call-start = ((), (), s32[]{:S(2)}) async-start(), calls=%async_computation.6 | async-start | bytes 1310720 | tf_op jit(solution)/shard_map/all_gather | solution.py:73
  218.9 4.1 copy-start.2
  218.9 8.0 copy-start.6
  223.4 18.2 %collective-permute-start.3 = (f32[512,512]{1,0:T(8,128)S(1)}, f32[512,512]{1,0:T(8,128)S(1)}, u32[]{:S(2)}, u32[]{:S(2)}) collective-permute-start(f32[512,512]{1,0:T(8,128)S(1)} %get-tuple-element.106), channel_id=1, source_target_pairs={{4,0},{8,4},{12,8},{16,12},{20,16},{24,20},{28,24},{32,28},{36,32}... | collective-permute-start | bytes 3145736 | tf_op jit(solution)/shard_map/ppermute | solution.py:12
  228.5 78.9 %collective-permute-start.4 = (f32[512,512]{1,0:T(8,128)S(1)}, f32[512,512]{1,0:T(8,128)}, u32[]{:S(2)}, u32[]{:S(2)}) collective-permute-start(f32[512,512]{1,0:T(8,128)S(1)} %pad_maximum_fusion), channel_id=1, source_target_pairs={{4,0},{8,4},{12,8},{16,12},{20,16},{24,20},{28,24},{32,28},{36,32}... | collective-permute-start | bytes 3145736 | tf_op jit(solution)/shard_map/ppermute | solution.py:12
  231.9 68.4 %collective-permute-start.2 = (f32[128,512]{1,0:T(8,128)}, f32[128,512]{1,0:T(8,128)}, u32[]{:S(2)}, u32[]{:S(2)}) collective-permute-start(f32[128,512]{1,0:T(8,128)} %fusion.103), channel_id=1, source_target_pairs={{0,4},{4,8},{8,12},{12,16},{16,20},{20,24},{24,28},{28,32},{32,36}... | collective-permute-start | bytes 786440 | tf_op jit(solution)/shard_map/ppermute | solution.py:12
  293.7 4.2 copy-start.7
  302.1 1.3 copy-start.3
  303.4 16.8 %all-to-all-start.1 = ((f32[4,128,512]{1,2,0:T(8,128)}), f32[4,128,512]{1,2,0:T(8,128)S(1)}, u32[]{:S(2)}, u32[]{:S(2)}) async-start(f32[4,128,512]{1,2,0:T(8,128)} %stack.7), calls=%async_computation.1 | async-start | bytes 2097152 | tf_op jit(solution)/shard_map/all_to_all | solution.py:70
  306.9 149.9 %all-gather.8.cloned.1.call-start = ((), (), s32[]{:S(2)}) async-start(), calls=%async_computation.4 | async-start | bytes 1310720 | tf_op jit(solution)/shard_map/all_gather | solution.py:73
  453.7 29.5 %collective-permute-start.6 = (f32[512,512]{1,0:T(8,128)}, f32[512,512]{1,0:T(8,128)}, u32[]{:S(2)}, u32[]{:S(2)}) collective-permute-start(f32[512,512]{1,0:T(8,128)} %get-tuple-element.104), channel_id=1, source_target_pairs={{8,0},{12,4},{16,8},{20,12},{24,16},{28,20},{32,24},{36,28},{40,32... | collective-permute-start | bytes 3145736 | tf_op jit(solution)/shard_map/ppermute | solution.py:12
  456.8 3.7 copy-start.1
  462.1 84.0 %collective-permute-start.7 = (f32[512,512]{1,0:T(8,128)S(1)}, f32[512,512]{1,0:T(8,128)}, u32[]{:S(2)}, u32[]{:S(2)}) collective-permute-start(f32[512,512]{1,0:T(8,128)S(1)} %pad_maximum_fusion.2), channel_id=1, source_target_pairs={{8,0},{12,4},{16,8},{20,12},{24,16},{28,20},{32,24},{36,28},{40,32... | collective-permute-start | bytes 3145736 | tf_op jit(solution)/shard_map/ppermute | solution.py:12
  466.7 72.6 %collective-permute-start.5 = (f32[128,512]{1,0:T(8,128)}, f32[128,512]{1,0:T(8,128)}, u32[]{:S(2)}, u32[]{:S(2)}) collective-permute-start(f32[128,512]{1,0:T(8,128)} %fusion.101), channel_id=1, source_target_pairs={{0,8},{4,12},{8,16},{12,20},{16,24},{20,28},{24,32},{28,36},{32,40... | collective-permute-start | bytes 786440 | tf_op jit(solution)/shard_map/ppermute | solution.py:12
  532.6 4.2 copy-start.9
  537.3 2.0 copy-start.4
  542.3 18.4 %all-to-all-start.2 = ((f32[4,128,512]{1,2,0:T(8,128)}), f32[4,128,512]{1,2,0:T(8,128)S(1)}, u32[]{:S(2)}, u32[]{:S(2)}) async-start(f32[4,128,512]{1,2,0:T(8,128)} %stack.8), calls=%async_computation.2 | async-start | bytes 2097152 | tf_op jit(solution)/shard_map/all_to_all | solution.py:70
  545.9 198.6 %all-gather.10.cloned.1.call-start = ((), (), s32[]{:S(2)}) async-start(), calls=%async_computation.5 | async-start | bytes 1310720 | tf_op jit(solution)/shard_map/all_gather | solution.py:73
  647.0 49.9 %collective-permute-start.9 = (f32[512,512]{1,0:T(8,128)}, f32[512,512]{1,0:T(8,128)S(1)}, u32[]{:S(2)}, u32[]{:S(2)}) collective-permute-start(f32[512,512]{1,0:T(8,128)} %get-tuple-element.102), channel_id=1, source_target_pairs={{16,0},{20,4},{24,8},{28,12},{32,16},{36,20},{40,24},{44,28},{48,3... | collective-permute-start | bytes 3145736 | tf_op jit(solution)/shard_map/ppermute | solution.py:12
  697.0 49.4 %copy-start.8 = (f32[4,128,128]{1,2,0:T(8,128)S(1)}, f32[4,128,128]{1,2,0:T(8,128)}, u32[]{:S(2)}) copy-start(f32[4,128,128]{1,2,0:T(8,128)} %custom-call.47) | copy-start | bytes 786436
  744.5 3.7 copy-start
  750.6 49.8 %collective-permute-start.10 = (f32[512,512]{1,0:T(8,128)S(1)}, f32[512,512]{1,0:T(8,128)S(1)}, u32[]{:S(2)}, u32[]{:S(2)}) collective-permute-start(f32[512,512]{1,0:T(8,128)S(1)} %pad_maximum_fusion.4), channel_id=1, source_target_pairs={{16,0},{20,4},{24,8},{28,12},{32,16},{36,20},{40,24},{44,28},{48,3... | collective-permute-start | bytes 3145736 | tf_op jit(solution)/shard_map/ppermute | solution.py:12
  753.7 15.4 %collective-permute-start.8 = (f32[128,512]{1,0:T(8,128)S(1)}, f32[128,512]{1,0:T(8,128)S(1)}, u32[]{:S(2)}, u32[]{:S(2)}) collective-permute-start(f32[128,512]{1,0:T(8,128)S(1)} %fusion.99), channel_id=1, source_target_pairs={{0,16},{4,20},{8,24},{12,28},{16,32},{20,36},{24,40},{28,44},{32,4... | collective-permute-start | bytes 786440 | tf_op jit(solution)/shard_map/ppermute | solution.py:12
Sparse Core Ops, SparseCore 0:
  21.9 42.0 all-gather.5
  74.5 30.3 all-gather.11
  310.4 27.9 all-gather.7
  549.1 28.7 all-gather.9
